TPU v7x, 256 devices: a whole 4x4x8 slice. The times are simulated.
256 devices in a mesh: seq: 8 (over x, core), head: 32 (over y, z).
Axes of the slice: x: 4, y: 4, z: 8, core: 2. Of those that a mesh axis runs over, the one named last changes fastest.
Arguments:
- queries: bfloat16 [32768, 4096], P(('seq', 'head')), may hold values from -4 to 4
- keys: bfloat16 [32768, 1024], P(('seq', 'head')), may hold values from -4 to 4
- values: bfloat16 [32768, 1024], P(('seq', 'head')), may hold values from -6 to 6
- modality: int32 [32768], P(('seq', 'head')), may hold values 0 or 1
- clip_lengths: int32 [128], replicated, may hold values from 1 to 512, 32768 in all
- query_gains: float32 [2, 4096], replicated, may hold values from 0.5 to 5.2
- key_gains: float32 [2, 1024], replicated, may hold values from 0.5 to 5.2
- out_grad: bfloat16 [32768, 4096], P(('seq', 'head')), may hold values from -6 to 6
Outputs:
- attended: bfloat16 [32768, 4096], P(('seq', 'head'))
- query_grad: bfloat16 [32768, 4096], P(('seq', 'head'))
- key_grad: bfloat16 [32768, 1024], P(('seq', 'head'))
- value_grad: bfloat16 [32768, 1024], P(('seq', 'head'))
- query_gain_grad: float32 [2, 4096], replicated
- key_gain_grad: float32 [2, 1024], replicated
Inputs may be any that keep to these rules, and one draw needn't show every extreme that they name: `clip_lengths`: the clips cover the 32768 positions end to end; some clip has exactly 512 positions.
All inputs are finite; a program needn't handle non-finite values. No bound on the sum of `modality` on one device may be relied on, other than what follows from the above.
Results may differ from a plain program's by a relative error of at most 0.025.
The roundings to bfloat16 on the way count: a program that leaves them out, or rounds other values in their place, can miss the bound.
Values may be sent and summed in bfloat16 or wider, within the bound.
No kernel may reach another device: no remote copies, remote signals or barrier semaphores. Data moves between devices by JAX's collectives and lax.ppermute only.
A program may use at most 128 MiB of HBM per device.

v0:
```python
import math
import jax
import jax.numpy as jnp
from jax import lax
from jax.sharding import PartitionSpec as P

HD = 128
MOST = 512
row_block = 512


def from_behind(value, axis, steps):
    count = lax.axis_size(axis)
    first, last = (max(0, -steps), min(count, count - steps))
    return lax.ppermute(value, axis, [(source, source + steps) for source in range(first, last)])


def clip_start(clip_lengths, positions):
    order = jnp.arange(clip_lengths.shape[0], dtype=jnp.int32)
    begins = jnp.sum(jnp.where(order[None, :] < order[:, None], clip_lengths[None, :], 0), axis=1)
    chosen = jnp.where(
        begins[None, :] <= positions[:, None], begins[None, :], jnp.zeros((), jnp.int32)
    )
    return jnp.max(chosen, axis=1)


def normalize(rows, modality, gains):
    count, width = rows.shape
    shaped = rows.astype(jnp.float32).reshape(count, width // HD, HD)
    factor = lax.rsqrt(jnp.mean(shaped * shaped, axis=2, keepdims=True) + 1e-06)
    unit = shaped * factor
    gain_rows = jnp.where(modality[:, None] == 1, gains[1][None, :], gains[0][None, :]).reshape(
        count, width // HD, HD
    )
    normed = (unit * gain_rows).astype(jnp.bfloat16).reshape(count, width)
    return (normed, unit, factor, gain_rows)


def unnormalize(grad_low, unit, factor, gain_rows, modality):
    count = unit.shape[0]
    shaped = grad_low.astype(jnp.float32).reshape(unit.shape)
    along = shaped * gain_rows
    back = factor * (along - unit * jnp.mean(along * unit, axis=2, keepdims=True))
    term = (shaped * unit).reshape(count, -1)
    choose = (modality[:, None] == jnp.arange(2, dtype=jnp.int32)[None, :]).astype(jnp.float32)
    gain_part = jnp.einsum("rm,rc->mc", choose, term, precision=lax.Precision.HIGHEST)
    return (back.reshape(count, -1).astype(jnp.bfloat16), gain_part)


def spread_heads(rows, kv_heads, repeat):
    count = rows.shape[0]
    return jnp.broadcast_to(
        rows.reshape(count, kv_heads, 1, HD), (count, kv_heads, repeat, HD)
    ).reshape(count, kv_heads * repeat, HD)


def fold_heads(rows, kv_heads, repeat):
    count = rows.shape[0]
    return jnp.sum(rows.reshape(count, kv_heads, repeat, HD), axis=2)


def attend(query_norm, key_ext, value_ext, grad_rows, first, starts, block):
    rows = query_norm.shape[0]
    reach = key_ext.shape[0] - rows
    span = block + reach
    scale = 1.0 / math.sqrt(query_norm.shape[2])
    offsets = jnp.arange(span, dtype=jnp.int32)
    inside = jnp.arange(block, dtype=jnp.int32)

    def visit(carry, index):
        key_acc, value_acc = carry
        begin = index * block
        query_pos = first + begin + inside
        key_pos = first + begin - reach + offsets
        allowed = (key_pos[None, :] >= starts[:, None]) & (key_pos[None, :] <= query_pos[:, None])
        scores = (
            jnp.einsum("qnd,knd->qnk", query_norm, key_ext, preferred_element_type=jnp.float32)
            * scale
        )
        scores = jnp.where(allowed[:, None, :], scores, jnp.float32(-1e30))
        top = jnp.max(scores, axis=2, keepdims=True)
        expo = jnp.exp(scores - top)
        probs = expo / jnp.sum(expo, axis=2, keepdims=True)
        probs_low = probs.astype(jnp.bfloat16)
        attended = jnp.einsum(
            "qnk,knd->qnd", probs_low, value_ext, preferred_element_type=jnp.float32
        ).astype(jnp.bfloat16)
        delta = jnp.sum(
            grad_rows.astype(jnp.float32) * attended.astype(jnp.float32), axis=2, keepdims=True
        )
        prob_grad = jnp.einsum(
            "qnd,knd->qnk", grad_rows, value_ext, preferred_element_type=jnp.float32
        )
        score_grad = (probs * (prob_grad - delta) * scale).astype(jnp.bfloat16)
        query_grad = jnp.einsum(
            "qnk,knd->qnd", score_grad, key_ext, preferred_element_type=jnp.float32
        ).astype(jnp.bfloat16)
        key_step = jnp.einsum(
            "qnk,qnd->knd", score_grad, query_norm, preferred_element_type=jnp.float32
        )
        value_step = jnp.einsum(
            "qnk,qnd->knd", probs_low, grad_rows, preferred_element_type=jnp.float32
        )
        key_acc = key_acc + key_step
        value_acc = value_acc + value_step
        return ((key_acc, value_acc), (attended, query_grad))

    zeros = jnp.zeros(key_ext.shape, jnp.float32)
    (key_acc, value_acc), (attended, query_grad) = lax.scan(
        visit, (zeros, zeros), jnp.arange(rows // block, dtype=jnp.int32)
    )
    heads, depth = (query_norm.shape[1], query_norm.shape[2])
    return (
        attended.reshape(rows, heads, depth),
        query_grad.reshape(rows, heads, depth),
        key_acc,
        value_acc,
    )


def on_device(queries, keys, values, modality, clip_lengths, query_gains, key_gains, out_grad):
    count, width = queries.shape
    heads = width // HD
    kv_heads = keys.shape[1] // HD
    repeat = heads // kv_heads
    query_norm, query_unit, query_factor, query_gain_rows = normalize(
        queries, modality, query_gains
    )
    key_norm, key_unit, key_factor, key_gain_rows = normalize(keys, modality, key_gains)
    first = lax.axis_index(("seq", "head")) * count
    depth = (MOST + count - 1) // count
    far_keys = []
    far_values = []
    for step in range(depth, 0, -1):
        moved_key, moved_value = from_behind((key_norm, values), ("seq", "head"), step)
        far_keys.append(moved_key)
        far_values.append(moved_value)
    key_ext = jnp.concatenate(far_keys + [key_norm], 0)
    value_ext = jnp.concatenate(far_values + [values], 0)
    starts = clip_start(clip_lengths, first + jnp.arange(count, dtype=jnp.int32))
    attended, query_low, key_acc, value_acc = attend(
        query_norm.reshape(count, heads, HD),
        spread_heads(key_ext, kv_heads, repeat),
        spread_heads(value_ext, kv_heads, repeat),
        out_grad.reshape(count, heads, HD),
        first,
        starts,
        min(row_block, count),
    )
    key_acc = fold_heads(key_acc, kv_heads, repeat)
    value_acc = fold_heads(value_acc, kv_heads, repeat)
    front_key = key_acc[:MOST]
    front_value = value_acc[:MOST]
    key_total = key_acc[MOST:]
    value_total = value_acc[MOST:]
    for step in range(depth, 0, -1):
        begin = (depth - step) * count
        back_key, back_value = (
            from_behind(
                front_key[begin : begin + count].astype(jnp.bfloat16), ("seq", "head"), -step
            ).astype(jnp.float32),
            from_behind(
                front_value[begin : begin + count].astype(jnp.bfloat16), ("seq", "head"), -step
            ).astype(jnp.float32),
        )
        key_total = key_total + back_key
        value_total = value_total + back_value
    attended = attended.reshape(count, width)
    query_low = query_low.reshape(count, width)
    key_low = key_total.reshape(count, kv_heads * HD).astype(jnp.bfloat16)
    value_grad = value_total.reshape(count, kv_heads * HD).astype(jnp.bfloat16)
    query_grad, query_gain = unnormalize(
        query_low, query_unit, query_factor, query_gain_rows, modality
    )
    key_grad, key_gain = unnormalize(key_low, key_unit, key_factor, key_gain_rows, modality)
    query_gain_grad, key_gain_grad = lax.psum((query_gain, key_gain), ("seq", "head"))
    return (attended, query_grad, key_grad, value_grad, query_gain_grad, key_gain_grad)


def solution(mesh):
    return jax.shard_map(
        on_device,
        mesh=mesh,
        in_specs=(
            P(("seq", "head"), None),
            P(("seq", "head"), None),
            P(("seq", "head"), None),
            P(("seq", "head")),
            P(),
            P(),
            P(),
            P(("seq", "head"), None),
        ),
        out_specs=(
            P(("seq", "head"), None),
            P(("seq", "head"), None),
            P(("seq", "head"), None),
            P(("seq", "head"), None),
            P(),
            P(),
        ),
        check_vma=False,
    )
```

profile of v0, /device:TPU:1, one launch (start us, length us, event | category | flops | bytes accessed | tf_op | source)
XLA Modules:
  0.0 338.0 jit_solution(9499922176696073550)
XLA Ops:
  0.7 5.9 %collective-permute-start.2 = (bf16[128,1024]{1,0:T(8,128)(2,1)}, bf16[128,1024]{1,0:T(8,128)(2,1)}, u32[]{:S(2)}, u32[]{:S(2)}) collective-permute-start(bf16[128,1024]{1,0:T(8,128)(2,1)} %param.10), channel_id=1, source_target_pairs={{0,2},{1,3},{2,4},{3,5},{4,6},{5,7},{6,8},{7,9},{8,10},{9,11},{10,... | collective-permute-start | bytes 786440 | tf_op jit(solution)/shard_map/ppermute | solution.py:15
  6.5 6.6 %collective-permute-start.1 = (bf16[128,1024]{1,0:T(8,128)(2,1)}, bf16[128,1024]{1,0:T(8,128)(2,1)}, u32[]{:S(2)}, u32[]{:S(2)}) collective-permute-start(bf16[128,1024]{1,0:T(8,128)(2,1)} %param.10), channel_id=1, source_target_pairs={{0,3},{1,4},{2,5},{3,6},{4,7},{5,8},{6,9},{7,10},{8,11},{9,12},{10... | collective-permute-start | bytes 786440 | tf_op jit(solution)/shard_map/ppermute | solution.py:15
  14.6 1.1 copy.65
  16.1 3.1 collective-permute-start.6
  19.2 2.7 collective-permute-start.5
  21.9 7.0 %collective-permute-start.4 = (bf16[128,1024]{1,0:T(8,128)(2,1)S(1)}, bf16[128,1024]{1,0:T(8,128)(2,1)}, u32[]{:S(2)}, u32[]{:S(2)}) collective-permute-start(bf16[128,1024]{1,0:T(8,128)(2,1)S(1)} %multiply_convert_fusion.1), channel_id=1, source_target_pairs={{0,4},{1,5},{2,6},{3,7},{4,8},{5,9},{6,10},{7,11},{8,12},{9,13},{1... | collective-permute-start | bytes 786440 | tf_op jit(solution)/shard_map/ppermute | solution.py:15
  29.2 1.5 copy.68
  31.8 2.3 copy.73
  34.8 42.1 %collective-permute-done.4 = bf16[128,1024]{1,0:T(8,128)(2,1)} collective-permute-done((bf16[128,1024]{1,0:T(8,128)(2,1)S(1)}, bf16[128,1024]{1,0:T(8,128)(2,1)}, u32[]{:S(2)}, u32[]{:S(2)}) %collective-permute-start.4) | collective-permute-done | bytes 262176 | tf_op jit(solution)/shard_map/ppermute | solution.py:15
  77.0 1.9 collective-permute-start.7
  78.9 1.0 copy.92
  80.6 1.9 collective-permute-start
  82.5 1.0 copy.94
  83.5 9.7 %collective-permute-start.3 = (bf16[128,1024]{1,0:T(8,128)(2,1)S(1)}, bf16[128,1024]{1,0:T(8,128)(2,1)}, u32[]{:S(2)}, u32[]{:S(2)}) collective-permute-start(bf16[128,1024]{1,0:T(8,128)(2,1)S(1)} %copy-done.9), channel_id=1, source_target_pairs={{0,1},{1,2},{2,3},{3,4},{4,5},{5,6},{6,7},{7,8},{8,9},{9,10},{10,1... | collective-permute-start | bytes 786440 | tf_op jit(solution)/shard_map/ppermute | solution.py:15
  97.9 2.8 copy.67
  100.7 1.7 constant_dynamic-update-slice_fusion.3
  102.4 1.8 constant_dynamic-update-slice_fusion.2
  104.1 4.2 %collective-permute-done.3 = bf16[128,1024]{1,0:T(8,128)(2,1)} collective-permute-done((bf16[128,1024]{1,0:T(8,128)(2,1)S(1)}, bf16[128,1024]{1,0:T(8,128)(2,1)}, u32[]{:S(2)}, u32[]{:S(2)}) %collective-permute-start.3) | collective-permute-done | bytes 262176 | tf_op jit(solution)/shard_map/ppermute | solution.py:15
  108.3 1.7 constant_dynamic-update-slice_fusion.1
  110.7 2.6 copy_bitcast_fusion
  113.3 3.1 broadcast_in_dim.164
  116.4 9.4 %fusion.39 = (f32[128,32]{0,1:T(8,128)S(1)}, f32[128,32,640]{0,2,1:T(8,128)}) fusion(pred[128,640]{0,1:T(8,128)(4,1)S(1)} %compare_and_fusion, bf16[640,32,128]{0,2,1:T(8,128)(2,1)} %bitcast.117, f32[128,4096]{0,1:T(8,128)S(1)} %copy.68, f32[32,128]{1,0:T(8,128)S(1)} %bitcast.140, f32[32,128]{1,0:T(8,128)S(1)} %bitcast.136, ...), kind=kOutput, calls=%fused_computation.79 | convolution fusion | flops 683672192 | bytes 17973376 | tf_op jit(solution)/shard_map/while/body/eval_jaxpr/sub | solution.py:82
  125.8 5.4 %fusion.8 = bf16[128,32,640]{0,2,1:T(8,128)(2,1)S(1)} fusion(f32[128,32,640]{0,2,1:T(8,128)} %get-tuple-element.88, f32[128,32]{0,1:T(8,128)S(1)} %get-tuple-element.87), kind=kLoop, calls=%fused_computation.14 | loop fusion | flops 5242880 | bytes 15745024 | tf_op jit(solution)/shard_map/while/body/eval_jaxpr/convert_element_type | solution.py:84
  131.2 1.2 broadcast_in_dim.154
  132.4 3.1 multiply_reduce_fusion
  135.5 3.4 %bitcast_reduce_fusion = f32[640,8,128]{2,0,1:T(8,128)} fusion(bf16[128,32,640]{0,2,1:T(8,128)(2,1)S(1)} %fusion.8, bf16[128,32,128]{0,2,1:T(8,128)(2,1)S(1)} %bitcast.121), kind=kOutput, calls=%fused_computation.1 | convolution fusion | flops 673054720 | bytes 8912896 | tf_op jit(solution)/shard_map/while/body/eval_jaxpr/qnk,qnd->knd/dot_general | solution.py:101
  138.9 6.8 %fusion.3 = bf16[128,32,640]{0,2,1:T(8,128)(2,1)} fusion(f32[128,32]{0,1:T(8,128)S(1)} %get-tuple-element.89, f32[128,32,640]{0,2,1:T(8,128)} %get-tuple-element.88, f32[128,32]{0,1:T(8,128)S(1)} %get-tuple-element.87, bf16[640,32,128]{2,0,1:T(8,128)(2,1)S(1)} %bitcast.115, bf16[128,32,128]{0,2,1:T(8,128)(2,1)S(1)} %bitcast.122), kind=kOutput, calls=%fused_computation.6 | convolution fusion | flops 684195840 | bytes 22052864 | tf_op jit(solution)/shard_map/while/body/eval_jaxpr/qnd,knd->qnk/dot_general | solution.py:91
  145.7 4.0 %fusion.12 = (f32[128,32]{0,1:T(8,128)S(1)}, bf16[32,128,128]{2,1,0:T(8,128)(2,1)S(1)}) fusion(f32[128,4096]{0,1:T(8,128)S(1)} %copy.68, f32[32,128]{1,0:T(8,128)S(1)} %bitcast.141, f32[32,128]{1,0:T(8,128)S(1)} %bitcast.137, f32[128,32]{0,1:T(8,128)S(1)} %add_rsqrt_fusion, pred[128]{0:T(512)(128)(4,1)S(1)} %broadcast_compare_fusion, ...), kind=kOutput, calls=%fused_computation.21 | convolution fusion | flops 674754560 | bytes 13697152 | tf_op jit(solution)/shard_map/while/body/eval_jaxpr/qnk,knd->qnd/dot_general | solution.py:95
  149.8 4.0 %bitcast_reduce_fusion.1 = f32[640,8,128]{0,2,1:T(8,128)} fusion(bf16[128,32,640]{0,2,1:T(8,128)(2,1)S(1)} %copy-done.2, f32[128,4096]{0,1:T(8,128)S(1)} %copy.68, f32[32,128]{1,0:T(8,128)S(1)} %bitcast.142, f32[32,128]{1,0:T(8,128)S(1)} %bitcast.138, f32[128,32]{0,1:T(8,128)S(1)} %add_rsqrt_fusion, pred[128]{0:T(512)(128)(4,1)S(1)} %broadcast_compare_fusion), kind=kOutput, calls=%fused_computation.2 | convolution fusion | flops 675151872 | bytes 10010752 | tf_op jit(solution)/shard_map/while/body/eval_jaxpr/qnk,qnd->knd/dot_general | solution.py:98
  153.8 2.5 bitcast_multiply_fusion
  156.3 2.4 copy.80
  158.7 2.3 copy.79
  161.4 4.3 %collective-permute-start.8 = (bf16[128,8,128]{0,2,1:T(8,128)(2,1)S(1)}, bf16[128,8,128]{0,2,1:T(8,128)(2,1)S(1)}, u32[]{:S(2)}, u32[]{:S(2)}) collective-permute-start(bf16[128,8,128]{0,2,1:T(8,128)(2,1)S(1)} %get-tuple-element.79), channel_id=1, source_target_pairs={{4,0},{5,1},{6,2},{7,3},{8,4},{9,5},{10,6},{11,7},{12,8},{13,9},{1... | collective-permute-start | bytes 786440 | tf_op jit(solution)/shard_map/ppermute | solution.py:15
  165.8 3.6 %collective-permute-start.11 = (bf16[128,8,128]{0,2,1:T(8,128)(2,1)S(1)}, bf16[128,8,128]{0,2,1:T(8,128)(2,1)S(1)}, u32[]{:S(2)}, u32[]{:S(2)}) collective-permute-start(bf16[128,8,128]{0,2,1:T(8,128)(2,1)S(1)} %get-tuple-element.80), channel_id=1, source_target_pairs={{1,0},{2,1},{3,2},{4,3},{5,4},{6,5},{7,6},{8,7},{9,8},{10,9},{11,1... | collective-permute-start | bytes 786440 | tf_op jit(solution)/shard_map/ppermute | solution.py:15
  169.4 8.8 %collective-permute-start.10 = (bf16[128,8,128]{0,2,1:T(8,128)(2,1)S(1)}, bf16[128,8,128]{0,2,1:T(8,128)(2,1)S(1)}, u32[]{:S(2)}, u32[]{:S(2)}) collective-permute-start(bf16[128,8,128]{0,2,1:T(8,128)(2,1)S(1)} %get-tuple-element.81), channel_id=1, source_target_pairs={{2,0},{3,1},{4,2},{5,3},{6,4},{7,5},{8,6},{9,7},{10,8},{11,9},{12,... | collective-permute-start | bytes 786440 | tf_op jit(solution)/shard_map/ppermute | solution.py:15
  178.3 6.0 %collective-permute-start.9 = (bf16[128,8,128]{0,2,1:T(8,128)(2,1)S(1)}, bf16[128,8,128]{0,2,1:T(8,128)(2,1)S(1)}, u32[]{:S(2)}, u32[]{:S(2)}) collective-permute-start(bf16[128,8,128]{0,2,1:T(8,128)(2,1)S(1)} %get-tuple-element.82), channel_id=1, source_target_pairs={{3,0},{4,1},{5,2},{6,3},{7,4},{8,5},{9,6},{10,7},{11,8},{12,9},{13... | collective-permute-start | bytes 786440 | tf_op jit(solution)/shard_map/ppermute | solution.py:15
  185.5 4.3 %collective-permute-start.12 = (bf16[128,8,128]{2,0,1:T(8,128)(2,1)}, bf16[128,8,128]{2,0,1:T(8,128)(2,1)S(1)}, u32[]{:S(2)}, u32[]{:S(2)}) collective-permute-start(bf16[128,8,128]{2,0,1:T(8,128)(2,1)} %get-tuple-element.75), channel_id=1, source_target_pairs={{4,0},{5,1},{6,2},{7,3},{8,4},{9,5},{10,6},{11,7},{12,8},{13,9},{1... | collective-permute-start | bytes 786440 | tf_op jit(solution)/shard_map/ppermute | solution.py:15
  189.8 1.1 fusion.28
  190.9 1.9 collective-permute-start.15
  192.9 2.5 collective-permute-start.14
  195.3 3.6 %collective-permute-done.10 = bf16[128,8,128]{0,2,1:T(8,128)(2,1)S(1)} collective-permute-done((bf16[128,8,128]{0,2,1:T(8,128)(2,1)S(1)}, bf16[128,8,128]{0,2,1:T(8,128)(2,1)S(1)}, u32[]{:S(2)}, u32[]{:S(2)}) %collective-permute-start.10) | collective-permute-done | bytes 262176 | tf_op jit(solution)/shard_map/ppermute | solution.py:15
  198.9 4.4 %collective-permute-start.13 = (bf16[128,8,128]{2,0,1:T(8,128)(2,1)}, bf16[128,8,128]{2,0,1:T(8,128)(2,1)}, u32[]{:S(2)}, u32[]{:S(2)}) collective-permute-start(bf16[128,8,128]{2,0,1:T(8,128)(2,1)} %get-tuple-element.78), channel_id=1, source_target_pairs={{3,0},{4,1},{5,2},{6,3},{7,4},{8,5},{9,6},{10,7},{11,8},{12,9},{13... | collective-permute-start | bytes 786440 | tf_op jit(solution)/shard_map/ppermute | solution.py:15
  203.3 13.8 %collective-permute-done.9 = bf16[128,8,128]{0,2,1:T(8,128)(2,1)S(1)} collective-permute-done((bf16[128,8,128]{0,2,1:T(8,128)(2,1)S(1)}, bf16[128,8,128]{0,2,1:T(8,128)(2,1)S(1)}, u32[]{:S(2)}, u32[]{:S(2)}) %collective-permute-start.9) | collective-permute-done | bytes 262176 | tf_op jit(solution)/shard_map/ppermute | solution.py:15
  217.1 1.0 convert_multiply_fusion
  220.1 11.8 %collective-permute-done.14 = bf16[128,8,128]{2,0,1:T(8,128)(2,1)} collective-permute-done((bf16[128,8,128]{2,0,1:T(8,128)(2,1)}, bf16[128,8,128]{2,0,1:T(8,128)(2,1)}, u32[]{:S(2)}, u32[]{:S(2)}) %collective-permute-start.14) | collective-permute-done | bytes 262176 | tf_op jit(solution)/shard_map/ppermute | solution.py:15
  231.9 14.3 %collective-permute-done.13 = bf16[128,8,128]{2,0,1:T(8,128)(2,1)} collective-permute-done((bf16[128,8,128]{2,0,1:T(8,128)(2,1)}, bf16[128,8,128]{2,0,1:T(8,128)(2,1)}, u32[]{:S(2)}, u32[]{:S(2)}) %collective-permute-start.13) | collective-permute-done | bytes 262176 | tf_op jit(solution)/shard_map/ppermute | solution.py:15
  246.2 1.4 fusion.18
  248.6 89.4 %all-reduce = (f32[2,4096]{1,0:T(2,128)}, f32[2,1024]{1,0:T(2,128)}) all-reduce(f32[2,4096]{1,0:T(2,128)S(1)} %fusion.28, f32[2,1024]{1,0:T(2,128)S(1)} %fusion.26), channel_id=1, replica_groups=mesh['seq'=8,'head'=32] {'seq','head'}, use_global_device_ids=true, to_apply=%region_11.12 | all-reduce | flops 10240 | bytes 81920 | tf_op jit(solution)/shard_map/psum | solution.py:176
  (78 shorter events, 14.7 us)
Async XLA Ops:
  0.6 15.3 %copy-start.8 = (bf16[128,1024]{1,0:T(8,128)(2,1)S(1)}, bf16[128,1024]{1,0:T(8,128)(2,1)}, u32[]{:S(2)}) copy-start(bf16[128,1024]{1,0:T(8,128)(2,1)} %param.9) | copy-start | bytes 786436
  0.6 28.3 %copy-start.12 = (s32[128]{0:T(128)S(1)}, s32[128]{0:T(128)}, u32[]{:S(2)}) copy-start(s32[128]{0:T(128)} %param.12) | copy-start | bytes 1540
  0.7 28.5 %copy-start.10 = (f32[2,4096]{1,0:T(2,128)S(1)}, f32[2,4096]{1,0:T(2,128)}, u32[]{:S(2)}) copy-start(f32[2,4096]{1,0:T(2,128)} %param.13) | copy-start | bytes 98308
  0.7 101.7 %collective-permute-start.2 = (bf16[128,1024]{1,0:T(8,128)(2,1)}, bf16[128,1024]{1,0:T(8,128)(2,1)}, u32[]{:S(2)}, u32[]{:S(2)}) collective-permute-start(bf16[128,1024]{1,0:T(8,128)(2,1)} %param.10), channel_id=1, source_target_pairs={{0,2},{1,3},{2,4},{3,5},{4,6},{5,7},{6,8},{7,9},{8,10},{9,11},{10,... | collective-permute-start | bytes 786440 | tf_op jit(solution)/shard_map/ppermute | solution.py:15
  6.5 94.2 %collective-permute-start.1 = (bf16[128,1024]{1,0:T(8,128)(2,1)}, bf16[128,1024]{1,0:T(8,128)(2,1)}, u32[]{:S(2)}, u32[]{:S(2)}) collective-permute-start(bf16[128,1024]{1,0:T(8,128)(2,1)} %param.10), channel_id=1, source_target_pairs={{0,3},{1,4},{2,5},{3,6},{4,7},{5,8},{6,9},{7,10},{8,11},{9,12},{10... | collective-permute-start | bytes 786440 | tf_op jit(solution)/shard_map/ppermute | solution.py:15
  16.1 64.5 %collective-permute-start.6 = (bf16[128,1024]{1,0:T(8,128)(2,1)S(1)}, bf16[128,1024]{1,0:T(8,128)(2,1)}, u32[]{:S(2)}, u32[]{:S(2)}) collective-permute-start(bf16[128,1024]{1,0:T(8,128)(2,1)S(1)} %multiply_convert_fusion.1), channel_id=1, source_target_pairs={{0,2},{1,3},{2,4},{3,5},{4,6},{5,7},{6,8},{7,9},{8,10},{9,11},{10,... | collective-permute-start | bytes 786440 | tf_op jit(solution)/shard_map/ppermute | solution.py:15
  19.2 64.3 %collective-permute-start.5 = (bf16[128,1024]{1,0:T(8,128)(2,1)S(1)}, bf16[128,1024]{1,0:T(8,128)(2,1)}, u32[]{:S(2)}, u32[]{:S(2)}) collective-permute-start(bf16[128,1024]{1,0:T(8,128)(2,1)S(1)} %multiply_convert_fusion.1), channel_id=1, source_target_pairs={{0,3},{1,4},{2,5},{3,6},{4,7},{5,8},{6,9},{7,10},{8,11},{9,12},{10... | collective-permute-start | bytes 786440 | tf_op jit(solution)/shard_map/ppermute | solution.py:15
  21.9 55.0 %collective-permute-start.4 = (bf16[128,1024]{1,0:T(8,128)(2,1)S(1)}, bf16[128,1024]{1,0:T(8,128)(2,1)}, u32[]{:S(2)}, u32[]{:S(2)}) collective-permute-start(bf16[128,1024]{1,0:T(8,128)(2,1)S(1)} %multiply_convert_fusion.1), channel_id=1, source_target_pairs={{0,4},{1,5},{2,6},{3,7},{4,8},{5,9},{6,10},{7,11},{8,12},{9,13},{1... | collective-permute-start | bytes 786440 | tf_op jit(solution)/shard_map/ppermute | solution.py:15
  31.8 48.8 %copy-start.9 = (bf16[128,1024]{1,0:T(8,128)(2,1)S(1)}, bf16[128,1024]{1,0:T(8,128)(2,1)}, u32[]{:S(2)}) copy-start(bf16[128,1024]{1,0:T(8,128)(2,1)} %param.10) | copy-start | bytes 786436
  77.0 18.7 %collective-permute-start.7 = (bf16[128,1024]{1,0:T(8,128)(2,1)S(1)}, bf16[128,1024]{1,0:T(8,128)(2,1)S(1)}, u32[]{:S(2)}, u32[]{:S(2)}) collective-permute-start(bf16[128,1024]{1,0:T(8,128)(2,1)S(1)} %multiply_convert_fusion.1), channel_id=1, source_target_pairs={{0,1},{1,2},{2,3},{3,4},{4,5},{5,6},{6,7},{7,8},{8,9},{9,10},{10,1... | collective-permute-start | bytes 786440 | tf_op jit(solution)/shard_map/ppermute | solution.py:15
  80.6 16.5 %collective-permute-start = (bf16[128,1024]{1,0:T(8,128)(2,1)S(1)}, bf16[128,1024]{1,0:T(8,128)(2,1)S(1)}, u32[]{:S(2)}, u32[]{:S(2)}) collective-permute-start(bf16[128,1024]{1,0:T(8,128)(2,1)S(1)} %copy-done.9), channel_id=1, source_target_pairs={{0,4},{1,5},{2,6},{3,7},{4,8},{5,9},{6,10},{7,11},{8,12},{9,13},{1... | collective-permute-start | bytes 786440 | tf_op jit(solution)/shard_map/ppermute | solution.py:15
  83.5 24.7 %collective-permute-start.3 = (bf16[128,1024]{1,0:T(8,128)(2,1)S(1)}, bf16[128,1024]{1,0:T(8,128)(2,1)}, u32[]{:S(2)}, u32[]{:S(2)}) collective-permute-start(bf16[128,1024]{1,0:T(8,128)(2,1)S(1)} %copy-done.9), channel_id=1, source_target_pairs={{0,1},{1,2},{2,3},{3,4},{4,5},{5,6},{6,7},{7,8},{8,9},{9,10},{10,1... | collective-permute-start | bytes 786440 | tf_op jit(solution)/shard_map/ppermute | solution.py:15
  102.3 11.0 %copy-start.3 = (bf16[640,8,128]{0,2,1:T(8,128)(2,1)S(1)}, bf16[640,8,128]{0,2,1:T(8,128)(2,1)}, u32[]{:S(2)}) copy-start(bf16[640,8,128]{0,2,1:T(8,128)(2,1)} %copy.67) | copy-start | bytes 3932164
  125.8 5.4 %copy-start.4 = (bf16[640,8,128]{2,0,1:T(8,128)(2,1)S(1)}, bf16[640,8,128]{2,0,1:T(8,128)(2,1)}, u32[]{:S(2)}) copy-start(bf16[640,8,128]{2,0,1:T(8,128)(2,1)} %copy_bitcast_fusion) | copy-start | bytes 3932164
  131.2 1.2 copy-start.5
  135.5 10.2 %slice-start = ((s8[5242880]{0:T(1024)(128)(4,1)}), s8[1048576]{0:T(1024)(128)(4,1)S(1)}, s32[]{:S(2)}) async-start(s8[5242880]{0:T(1024)(128)(4,1)} %bitcast.118), calls=%async_computation | async-start | bytes 2097152
  138.9 6.8 %slice-start.1 = ((s8[5242880]{0:T(1024)(128)(4,1)}), s8[4194304]{0:T(1024)(128)(4,1)S(1)}, s32[]{:S(2)}) async-start(s8[5242880]{0:T(1024)(128)(4,1)} %bitcast.118), calls=%async_computation.1 | async-start | bytes 8388608
  145.7 4.1 %copy-start.2 = (bf16[128,32,640]{0,2,1:T(8,128)(2,1)S(1)}, bf16[128,32,640]{0,2,1:T(8,128)(2,1)}, u32[]{:S(2)}) copy-start(bf16[128,32,640]{0,2,1:T(8,128)(2,1)} %fusion.3) | copy-start | bytes 15728644
  156.3 4.7 %copy-start = (f32[640,8,128]{0,2,1:T(8,128)S(1)}, f32[640,8,128]{0,2,1:T(8,128)}, u32[]{:S(2)}) copy-start(f32[640,8,128]{0,2,1:T(8,128)} %bitcast_reduce_fusion.1) | copy-start | bytes 7864324
  161.0 23.3 %copy-start.6 = (f32[640,8,128]{2,0,1:T(8,128)S(1)}, f32[640,8,128]{2,0,1:T(8,128)}, u32[]{:S(2)}) copy-start(f32[640,8,128]{2,0,1:T(8,128)} %bitcast_reduce_fusion) | copy-start | bytes 7864324
  161.4 29.5 %collective-permute-start.8 = (bf16[128,8,128]{0,2,1:T(8,128)(2,1)S(1)}, bf16[128,8,128]{0,2,1:T(8,128)(2,1)S(1)}, u32[]{:S(2)}, u32[]{:S(2)}) collective-permute-start(bf16[128,8,128]{0,2,1:T(8,128)(2,1)S(1)} %get-tuple-element.79), channel_id=1, source_target_pairs={{4,0},{5,1},{6,2},{7,3},{8,4},{9,5},{10,6},{11,7},{12,8},{13,9},{1... | collective-permute-start | bytes 786440 | tf_op jit(solution)/shard_map/ppermute | solution.py:15
  165.8 27.1 %collective-permute-start.11 = (bf16[128,8,128]{0,2,1:T(8,128)(2,1)S(1)}, bf16[128,8,128]{0,2,1:T(8,128)(2,1)S(1)}, u32[]{:S(2)}, u32[]{:S(2)}) collective-permute-start(bf16[128,8,128]{0,2,1:T(8,128)(2,1)S(1)} %get-tuple-element.80), channel_id=1, source_target_pairs={{1,0},{2,1},{3,2},{4,3},{5,4},{6,5},{7,6},{8,7},{9,8},{10,9},{11,1... | collective-permute-start | bytes 786440 | tf_op jit(solution)/shard_map/ppermute | solution.py:15
  169.4 29.5 %collective-permute-start.10 = (bf16[128,8,128]{0,2,1:T(8,128)(2,1)S(1)}, bf16[128,8,128]{0,2,1:T(8,128)(2,1)S(1)}, u32[]{:S(2)}, u32[]{:S(2)}) collective-permute-start(bf16[128,8,128]{0,2,1:T(8,128)(2,1)S(1)} %get-tuple-element.81), channel_id=1, source_target_pairs={{2,0},{3,1},{4,2},{5,3},{6,4},{7,5},{8,6},{9,7},{10,8},{11,9},{12,... | collective-permute-start | bytes 786440 | tf_op jit(solution)/shard_map/ppermute | solution.py:15
  178.2 11.6 %copy-start.1 = (f32[128,32,128]{0,2,1:T(8,128)S(1)}, f32[128,32,128]{0,2,1:T(8,128)}, u32[]{:S(2)}) copy-start(f32[128,32,128]{0,2,1:T(8,128)} %get-tuple-element.73) | copy-start | bytes 6291460
  178.3 11.6 %copy-start.11 = (s32[128]{0:T(128)S(1)}, s32[128]{0:T(128)}, u32[]{:S(2)}) copy-start(s32[128]{0:T(128)} %param.11) | copy-start | bytes 1540
  178.3 38.8 %collective-permute-start.9 = (bf16[128,8,128]{0,2,1:T(8,128)(2,1)S(1)}, bf16[128,8,128]{0,2,1:T(8,128)(2,1)S(1)}, u32[]{:S(2)}, u32[]{:S(2)}) collective-permute-start(bf16[128,8,128]{0,2,1:T(8,128)(2,1)S(1)} %get-tuple-element.82), channel_id=1, source_target_pairs={{3,0},{4,1},{5,2},{6,3},{7,4},{8,5},{9,6},{10,7},{11,8},{12,9},{13... | collective-permute-start | bytes 786440 | tf_op jit(solution)/shard_map/ppermute | solution.py:15
  185.5 34.6 %collective-permute-start.12 = (bf16[128,8,128]{2,0,1:T(8,128)(2,1)}, bf16[128,8,128]{2,0,1:T(8,128)(2,1)S(1)}, u32[]{:S(2)}, u32[]{:S(2)}) collective-permute-start(bf16[128,8,128]{2,0,1:T(8,128)(2,1)} %get-tuple-element.75), channel_id=1, source_target_pairs={{4,0},{5,1},{6,2},{7,3},{8,4},{9,5},{10,6},{11,7},{12,8},{13,9},{1... | collective-permute-start | bytes 786440 | tf_op jit(solution)/shard_map/ppermute | solution.py:15
  190.9 29.2 %collective-permute-start.15 = (bf16[128,8,128]{2,0,1:T(8,128)(2,1)}, bf16[128,8,128]{2,0,1:T(8,128)(2,1)}, u32[]{:S(2)}, u32[]{:S(2)}) collective-permute-start(bf16[128,8,128]{2,0,1:T(8,128)(2,1)} %get-tuple-element.76), channel_id=1, source_target_pairs={{1,0},{2,1},{3,2},{4,3},{5,4},{6,5},{7,6},{8,7},{9,8},{10,9},{11,1... | collective-permute-start | bytes 786440 | tf_op jit(solution)/shard_map/ppermute | solution.py:15
  192.9 39.0 %collective-permute-start.14 = (bf16[128,8,128]{2,0,1:T(8,128)(2,1)}, bf16[128,8,128]{2,0,1:T(8,128)(2,1)}, u32[]{:S(2)}, u32[]{:S(2)}) collective-permute-start(bf16[128,8,128]{2,0,1:T(8,128)(2,1)} %get-tuple-element.77), channel_id=1, source_target_pairs={{2,0},{3,1},{4,2},{5,3},{6,4},{7,5},{8,6},{9,7},{10,8},{11,9},{12,... | collective-permute-start | bytes 786440 | tf_op jit(solution)/shard_map/ppermute | solution.py:15
  198.9 47.2 %collective-permute-start.13 = (bf16[128,8,128]{2,0,1:T(8,128)(2,1)}, bf16[128,8,128]{2,0,1:T(8,128)(2,1)}, u32[]{:S(2)}, u32[]{:S(2)}) collective-permute-start(bf16[128,8,128]{2,0,1:T(8,128)(2,1)} %get-tuple-element.78), channel_id=1, source_target_pairs={{3,0},{4,1},{5,2},{6,3},{7,4},{8,5},{9,6},{10,7},{11,8},{12,9},{13... | collective-permute-start | bytes 786440 | tf_op jit(solution)/shard_map/ppermute | solution.py:15
  218.1 1.6 copy-start.7
where the time goes:
time: 339 us; the launch traced here: 338 us
  waiting for transfers between devices  89.8 us (26%)
  blocking collectives  89.4 us (26%)
  starting transfers between devices  74.7 us (22%)
  local copies, waits for them, and re-layouts  36.7 us (11%)
  matrix products  32.2 us (9%)
  other arithmetic  14.2 us (4%)
    ppermute x16, waiting for transfers between devices, from_behind(): lax.ppermute(value, axis, [(source, source + steps) for source in range(f...  89.8 us
    psum x1, blocking collectives, on_device(): lax.psum((query_gain, key_gain), ('seq', 'head'))  89.4 us
    ppermute x16, starting transfers between devices, from_behind(): lax.ppermute(value, axis, [(source, source + steps) for source in range(f...  74.7 us
    unnamed x48, local copies, waits for them, and re-layouts  20.5 us
    broadcast_in_dim x4, local copies, waits for them, and re-layouts, spread_heads(): jnp.broadcast_to(rows.reshape(count, kv_heads, 1, HD), (count, kv_heads,...  9.7 us
    sub x1, matrix products, visit(): expo = jnp.exp(scores - top)  9.41 us
  transfers between devices with their start and end apart: 16, of which 6 were waited for; matrix products, arithmetic and copies ran while one was open for 8% of the time, Pallas kernels for 0%

commit v1 on v0

--- a/solution.py
+++ b/solution.py
@@ -173,7 +173,7 @@
         query_low, query_unit, query_factor, query_gain_rows, modality
     )
     key_grad, key_gain = unnormalize(key_low, key_unit, key_factor, key_gain_rows, modality)
-    query_gain_grad, key_gain_grad = lax.psum((query_gain, key_gain), ("seq", "head"))
+    query_gain_grad, key_gain_grad = lax.psum(lax.psum((query_gain, key_gain), "head"), "seq")
     return (attended, query_grad, key_grad, value_grad, query_gain_grad, key_gain_grad)
 
 

time: 339 us -> 426 us (1.26)
  blocking collectives: 89.4 us -> 177 us
    psum x1 -> x2, blocking collectives: 89.4 us -> 177 us  [the longest x1 128 us: on_device(): lax.psum((query_gain, key_gain), 'head')]
  transfers between devices with their start and end apart: 16 -> 16, of which waited for: 6 -> 6; matrix products, arithmetic and copies ran while one was open for 8% -> 6% of each run, Pallas kernels for 0% -> 0%
where the time goes in v1:
time: 426 us; the launch traced here: 425 us
  blocking collectives  177 us (42%)
  waiting for transfers between devices  89.8 us (21%)
  starting transfers between devices  74.6 us (18%)
  local copies, waits for them, and re-layouts  36.7 us (9%)
  matrix products  32.1 us (8%)
  other arithmetic  14.2 us (3%)
    psum x1, blocking collectives, on_device(): lax.psum((query_gain, key_gain), 'head')  128 us
    ppermute x16, waiting for transfers between devices, from_behind(): lax.ppermute(value, axis, [(source, source + steps) for source in range(f...  89.8 us
    ppermute x16, starting transfers between devices, from_behind(): lax.ppermute(value, axis, [(source, source + steps) for source in range(f...  74.6 us
    psum x1, blocking collectives, on_device(): lax.psum(lax.psum((query_gain, key_gain), 'head'), 'seq')  48.8 us
    unnamed x48, local copies, waits for them, and re-layouts  20.6 us
    broadcast_in_dim x4, local copies, waits for them, and re-layouts, spread_heads(): jnp.broadcast_to(rows.reshape(count, kv_heads, 1, HD), (count, kv_heads,...  9.67 us
    sub x1, matrix products, visit(): expo = jnp.exp(scores - top)  9.42 us
  transfers between devices with their start and end apart: 16, of which 6 were waited for; matrix products, arithmetic and copies ran while one was open for 6% of the time, Pallas kernels for 0%

profile of v1, /device:TPU:1, one launch (start us, length us, event | category | flops | bytes accessed | tf_op | source)
XLA Modules:
  0.0 425.3 jit_solution(9808279294980963115)
XLA Ops:
  0.7 5.9 %collective-permute-start.2 = (bf16[128,1024]{1,0:T(8,128)(2,1)}, bf16[128,1024]{1,0:T(8,128)(2,1)}, u32[]{:S(2)}, u32[]{:S(2)}) collective-permute-start(bf16[128,1024]{1,0:T(8,128)(2,1)} %param.10), channel_id=1, source_target_pairs={{0,2},{1,3},{2,4},{3,5},{4,6},{5,7},{6,8},{7,9},{8,10},{9,11},{10,... | collective-permute-start | bytes 786440 | tf_op jit(solution)/shard_map/ppermute | solution.py:15
  6.5 6.6 %collective-permute-start.1 = (bf16[128,1024]{1,0:T(8,128)(2,1)}, bf16[128,1024]{1,0:T(8,128)(2,1)}, u32[]{:S(2)}, u32[]{:S(2)}) collective-permute-start(bf16[128,1024]{1,0:T(8,128)(2,1)} %param.10), channel_id=1, source_target_pairs={{0,3},{1,4},{2,5},{3,6},{4,7},{5,8},{6,9},{7,10},{8,11},{9,12},{10... | collective-permute-start | bytes 786440 | tf_op jit(solution)/shard_map/ppermute | solution.py:15
  14.6 1.1 copy.65
  16.1 3.1 collective-permute-start.6
  19.2 2.7 collective-permute-start.5
  21.9 7.0 %collective-permute-start.4 = (bf16[128,1024]{1,0:T(8,128)(2,1)S(1)}, bf16[128,1024]{1,0:T(8,128)(2,1)}, u32[]{:S(2)}, u32[]{:S(2)}) collective-permute-start(bf16[128,1024]{1,0:T(8,128)(2,1)S(1)} %multiply_convert_fusion.1), channel_id=1, source_target_pairs={{0,4},{1,5},{2,6},{3,7},{4,8},{5,9},{6,10},{7,11},{8,12},{9,13},{1... | collective-permute-start | bytes 786440 | tf_op jit(solution)/shard_map/ppermute | solution.py:15
  29.2 1.5 copy.68
  31.8 2.3 copy.73
  34.8 42.1 %collective-permute-done.4 = bf16[128,1024]{1,0:T(8,128)(2,1)} collective-permute-done((bf16[128,1024]{1,0:T(8,128)(2,1)S(1)}, bf16[128,1024]{1,0:T(8,128)(2,1)}, u32[]{:S(2)}, u32[]{:S(2)}) %collective-permute-start.4) | collective-permute-done | bytes 262176 | tf_op jit(solution)/shard_map/ppermute | solution.py:15
  77.0 1.9 collective-permute-start.7
  80.6 1.9 collective-permute-start
  83.5 9.7 %collective-permute-start.3 = (bf16[128,1024]{1,0:T(8,128)(2,1)S(1)}, bf16[128,1024]{1,0:T(8,128)(2,1)}, u32[]{:S(2)}, u32[]{:S(2)}) collective-permute-start(bf16[128,1024]{1,0:T(8,128)(2,1)S(1)} %copy-done.9), channel_id=1, source_target_pairs={{0,1},{1,2},{2,3},{3,4},{4,5},{5,6},{6,7},{7,8},{8,9},{9,10},{10,1... | collective-permute-start | bytes 786440 | tf_op jit(solution)/shard_map/ppermute | solution.py:15
  93.2 1.0 copy.93
  97.9 2.8 copy.67
  100.7 1.7 constant_dynamic-update-slice_fusion.3
  102.3 1.8 constant_dynamic-update-slice_fusion.2
  104.1 4.2 collective-permute-done.3
  108.3 1.7 constant_dynamic-update-slice_fusion.1
  110.7 2.6 copy_bitcast_fusion
  113.3 3.1 broadcast_in_dim.164
  116.4 9.4 %fusion.39 = (f32[128,32]{0,1:T(8,128)S(1)}, f32[128,32,640]{0,2,1:T(8,128)}) fusion(pred[128,640]{0,1:T(8,128)(4,1)S(1)} %compare_and_fusion, bf16[640,32,128]{0,2,1:T(8,128)(2,1)} %bitcast.117, f32[128,4096]{0,1:T(8,128)S(1)} %copy.68, f32[32,128]{1,0:T(8,128)S(1)} %bitcast.140, f32[32,128]{1,0:T(8,128)S(1)} %bitcast.136, ...), kind=kOutput, calls=%fused_computation.79 | convolution fusion | flops 683672192 | bytes 17973376 | tf_op jit(solution)/shard_map/while/body/eval_jaxpr/sub | solution.py:82
  125.8 5.4 %fusion.8 = bf16[128,32,640]{0,2,1:T(8,128)(2,1)S(1)} fusion(f32[128,32,640]{0,2,1:T(8,128)} %get-tuple-element.90, f32[128,32]{0,1:T(8,128)S(1)} %get-tuple-element.89), kind=kLoop, calls=%fused_computation.14 | loop fusion | flops 5242880 | bytes 15745024 | tf_op jit(solution)/shard_map/while/body/eval_jaxpr/convert_element_type | solution.py:84
  131.2 1.2 broadcast_in_dim.154
  132.4 3.1 multiply_reduce_fusion
  135.5 3.4 bitcast_reduce_fusion
  138.9 6.8 %fusion.3 = bf16[128,32,640]{0,2,1:T(8,128)(2,1)} fusion(f32[128,32]{0,1:T(8,128)S(1)} %get-tuple-element.91, f32[128,32,640]{0,2,1:T(8,128)} %get-tuple-element.90, f32[128,32]{0,1:T(8,128)S(1)} %get-tuple-element.89, bf16[640,32,128]{2,0,1:T(8,128)(2,1)S(1)} %bitcast.115, bf16[128,32,128]{0,2,1:T(8,128)(2,1)S(1)} %bitcast.122), kind=kOutput, calls=%fused_computation.6 | convolution fusion | flops 684195840 | bytes 22052864 | tf_op jit(solution)/shard_map/while/body/eval_jaxpr/qnd,knd->qnk/dot_general | solution.py:91
  145.7 4.0 fusion.12
  149.7 4.0 bitcast_reduce_fusion.1
  153.7 2.5 bitcast_multiply_fusion
  156.2 2.4 copy.80
  158.7 2.3 copy.79
  161.4 4.3 %collective-permute-start.8 = (bf16[128,8,128]{0,2,1:T(8,128)(2,1)S(1)}, bf16[128,8,128]{0,2,1:T(8,128)(2,1)S(1)}, u32[]{:S(2)}, u32[]{:S(2)}) collective-permute-start(bf16[128,8,128]{0,2,1:T(8,128)(2,1)S(1)} %get-tuple-element.81), channel_id=1, source_target_pairs={{4,0},{5,1},{6,2},{7,3},{8,4},{9,5},{10,6},{11,7},{12,8},{13,9},{1... | collective-permute-start | bytes 786440 | tf_op jit(solution)/shard_map/ppermute | solution.py:15
  165.7 3.7 collective-permute-start.11
  169.4 8.8 %collective-permute-start.10 = (bf16[128,8,128]{0,2,1:T(8,128)(2,1)S(1)}, bf16[128,8,128]{0,2,1:T(8,128)(2,1)S(1)}, u32[]{:S(2)}, u32[]{:S(2)}) collective-permute-start(bf16[128,8,128]{0,2,1:T(8,128)(2,1)S(1)} %get-tuple-element.83), channel_id=1, source_target_pairs={{2,0},{3,1},{4,2},{5,3},{6,4},{7,5},{8,6},{9,7},{10,8},{11,9},{12,... | collective-permute-start | bytes 786440 | tf_op jit(solution)/shard_map/ppermute | solution.py:15
  178.2 6.0 %collective-permute-start.9 = (bf16[128,8,128]{0,2,1:T(8,128)(2,1)S(1)}, bf16[128,8,128]{0,2,1:T(8,128)(2,1)S(1)}, u32[]{:S(2)}, u32[]{:S(2)}) collective-permute-start(bf16[128,8,128]{0,2,1:T(8,128)(2,1)S(1)} %get-tuple-element.84), channel_id=1, source_target_pairs={{3,0},{4,1},{5,2},{6,3},{7,4},{8,5},{9,6},{10,7},{11,8},{12,9},{13... | collective-permute-start | bytes 786440 | tf_op jit(solution)/shard_map/ppermute | solution.py:15
  185.4 4.3 %collective-permute-start.12 = (bf16[128,8,128]{2,0,1:T(8,128)(2,1)}, bf16[128,8,128]{2,0,1:T(8,128)(2,1)S(1)}, u32[]{:S(2)}, u32[]{:S(2)}) collective-permute-start(bf16[128,8,128]{2,0,1:T(8,128)(2,1)} %get-tuple-element.77), channel_id=1, source_target_pairs={{4,0},{5,1},{6,2},{7,3},{8,4},{9,5},{10,6},{11,7},{12,8},{13,9},{1... | collective-permute-start | bytes 786440 | tf_op jit(solution)/shard_map/ppermute | solution.py:15
  189.8 1.1 fusion.28
  190.9 1.9 collective-permute-start.15
  192.8 2.5 collective-permute-start.14
  195.3 3.6 collective-permute-done.10
  198.9 4.3 %collective-permute-start.13 = (bf16[128,8,128]{2,0,1:T(8,128)(2,1)}, bf16[128,8,128]{2,0,1:T(8,128)(2,1)}, u32[]{:S(2)}, u32[]{:S(2)}) collective-permute-start(bf16[128,8,128]{2,0,1:T(8,128)(2,1)} %get-tuple-element.80), channel_id=1, source_target_pairs={{3,0},{4,1},{5,2},{6,3},{7,4},{8,5},{9,6},{10,7},{11,8},{12,9},{13... | collective-permute-start | bytes 786440 | tf_op jit(solution)/shard_map/ppermute | solution.py:15
  203.2 13.9 %collective-permute-done.9 = bf16[128,8,128]{0,2,1:T(8,128)(2,1)S(1)} collective-permute-done((bf16[128,8,128]{0,2,1:T(8,128)(2,1)S(1)}, bf16[128,8,128]{0,2,1:T(8,128)(2,1)S(1)}, u32[]{:S(2)}, u32[]{:S(2)}) %collective-permute-start.9) | collective-permute-done | bytes 262176 | tf_op jit(solution)/shard_map/ppermute | solution.py:15
  217.1 1.0 convert_multiply_fusion
  220.1 11.8 %collective-permute-done.14 = bf16[128,8,128]{2,0,1:T(8,128)(2,1)} collective-permute-done((bf16[128,8,128]{2,0,1:T(8,128)(2,1)}, bf16[128,8,128]{2,0,1:T(8,128)(2,1)}, u32[]{:S(2)}, u32[]{:S(2)}) %collective-permute-start.14) | collective-permute-done | bytes 262176 | tf_op jit(solution)/shard_map/ppermute | solution.py:15
  231.8 14.3 %collective-permute-done.13 = bf16[128,8,128]{2,0,1:T(8,128)(2,1)} collective-permute-done((bf16[128,8,128]{2,0,1:T(8,128)(2,1)}, bf16[128,8,128]{2,0,1:T(8,128)(2,1)}, u32[]{:S(2)}, u32[]{:S(2)}) %collective-permute-start.13) | collective-permute-done | bytes 262176 | tf_op jit(solution)/shard_map/ppermute | solution.py:15
  246.1 1.4 fusion.18
  248.6 127.9 %all-reduce = (f32[2,4096]{1,0:T(2,128)S(1)}, f32[2,1024]{1,0:T(2,128)S(1)}) all-reduce(f32[2,4096]{1,0:T(2,128)S(1)} %fusion.28, f32[2,1024]{1,0:T(2,128)S(1)} %fusion.26), channel_id=1, replica_groups=mesh['seq'=8,'head'=32] {'head'}, use_global_device_ids=true, to_apply=%region_11.12 | all-reduce | flops 10240 | bytes 81920 | tf_op jit(solution)/shard_map/psum | solution.py:176
  376.5 48.8 %all-reduce.1 = (f32[2,4096]{1,0:T(2,128)}, f32[2,1024]{1,0:T(2,128)}) all-reduce(f32[2,4096]{1,0:T(2,128)S(1)} %get-tuple-element.69, f32[2,1024]{1,0:T(2,128)S(1)} %get-tuple-element.70), channel_id=1, replica_groups=mesh['seq'=8,'head'=32] {'seq'}, use_global_device_ids=true, to_apply=%region_12.13 | all-reduce | flops 10240 | bytes 81920 | tf_op jit(solution)/shard_map/psum | solution.py:176
  (79 shorter events, 15.7 us)
Async XLA Ops:
  0.6 15.3 %copy-start.8 = (bf16[128,1024]{1,0:T(8,128)(2,1)S(1)}, bf16[128,1024]{1,0:T(8,128)(2,1)}, u32[]{:S(2)}) copy-start(bf16[128,1024]{1,0:T(8,128)(2,1)} %param.9) | copy-start | bytes 786436
  0.6 28.3 %copy-start.12 = (s32[128]{0:T(128)S(1)}, s32[128]{0:T(128)}, u32[]{:S(2)}) copy-start(s32[128]{0:T(128)} %param.12) | copy-start | bytes 1540
  0.7 28.5 %copy-start.10 = (f32[2,4096]{1,0:T(2,128)S(1)}, f32[2,4096]{1,0:T(2,128)}, u32[]{:S(2)}) copy-start(f32[2,4096]{1,0:T(2,128)} %param.13) | copy-start | bytes 98308
  0.7 101.7 %collective-permute-start.2 = (bf16[128,1024]{1,0:T(8,128)(2,1)}, bf16[128,1024]{1,0:T(8,128)(2,1)}, u32[]{:S(2)}, u32[]{:S(2)}) collective-permute-start(bf16[128,1024]{1,0:T(8,128)(2,1)} %param.10), channel_id=1, source_target_pairs={{0,2},{1,3},{2,4},{3,5},{4,6},{5,7},{6,8},{7,9},{8,10},{9,11},{10,... | collective-permute-start | bytes 786440 | tf_op jit(solution)/shard_map/ppermute | solution.py:15
  6.5 94.1 %collective-permute-start.1 = (bf16[128,1024]{1,0:T(8,128)(2,1)}, bf16[128,1024]{1,0:T(8,128)(2,1)}, u32[]{:S(2)}, u32[]{:S(2)}) collective-permute-start(bf16[128,1024]{1,0:T(8,128)(2,1)} %param.10), channel_id=1, source_target_pairs={{0,3},{1,4},{2,5},{3,6},{4,7},{5,8},{6,9},{7,10},{8,11},{9,12},{10... | collective-permute-start | bytes 786440 | tf_op jit(solution)/shard_map/ppermute | solution.py:15
  16.1 64.5 %collective-permute-start.6 = (bf16[128,1024]{1,0:T(8,128)(2,1)S(1)}, bf16[128,1024]{1,0:T(8,128)(2,1)}, u32[]{:S(2)}, u32[]{:S(2)}) collective-permute-start(bf16[128,1024]{1,0:T(8,128)(2,1)S(1)} %multiply_convert_fusion.1), channel_id=1, source_target_pairs={{0,2},{1,3},{2,4},{3,5},{4,6},{5,7},{6,8},{7,9},{8,10},{9,11},{10,... | collective-permute-start | bytes 786440 | tf_op jit(solution)/shard_map/ppermute | solution.py:15
  19.2 64.3 %collective-permute-start.5 = (bf16[128,1024]{1,0:T(8,128)(2,1)S(1)}, bf16[128,1024]{1,0:T(8,128)(2,1)}, u32[]{:S(2)}, u32[]{:S(2)}) collective-permute-start(bf16[128,1024]{1,0:T(8,128)(2,1)S(1)} %multiply_convert_fusion.1), channel_id=1, source_target_pairs={{0,3},{1,4},{2,5},{3,6},{4,7},{5,8},{6,9},{7,10},{8,11},{9,12},{10... | collective-permute-start | bytes 786440 | tf_op jit(solution)/shard_map/ppermute | solution.py:15
  21.9 55.0 %collective-permute-start.4 = (bf16[128,1024]{1,0:T(8,128)(2,1)S(1)}, bf16[128,1024]{1,0:T(8,128)(2,1)}, u32[]{:S(2)}, u32[]{:S(2)}) collective-permute-start(bf16[128,1024]{1,0:T(8,128)(2,1)S(1)} %multiply_convert_fusion.1), channel_id=1, source_target_pairs={{0,4},{1,5},{2,6},{3,7},{4,8},{5,9},{6,10},{7,11},{8,12},{9,13},{1... | collective-permute-start | bytes 786440 | tf_op jit(solution)/shard_map/ppermute | solution.py:15
  31.8 48.8 %copy-start.9 = (bf16[128,1024]{1,0:T(8,128)(2,1)S(1)}, bf16[128,1024]{1,0:T(8,128)(2,1)}, u32[]{:S(2)}) copy-start(bf16[128,1024]{1,0:T(8,128)(2,1)} %param.10) | copy-start | bytes 786436
  77.0 18.7 %collective-permute-start.7 = (bf16[128,1024]{1,0:T(8,128)(2,1)S(1)}, bf16[128,1024]{1,0:T(8,128)(2,1)S(1)}, u32[]{:S(2)}, u32[]{:S(2)}) collective-permute-start(bf16[128,1024]{1,0:T(8,128)(2,1)S(1)} %multiply_convert_fusion.1), channel_id=1, source_target_pairs={{0,1},{1,2},{2,3},{3,4},{4,5},{5,6},{6,7},{7,8},{8,9},{9,10},{10,1... | collective-permute-start | bytes 786440 | tf_op jit(solution)/shard_map/ppermute | solution.py:15
  80.6 16.5 %collective-permute-start = (bf16[128,1024]{1,0:T(8,128)(2,1)S(1)}, bf16[128,1024]{1,0:T(8,128)(2,1)S(1)}, u32[]{:S(2)}, u32[]{:S(2)}) collective-permute-start(bf16[128,1024]{1,0:T(8,128)(2,1)S(1)} %copy-done.9), channel_id=1, source_target_pairs={{0,4},{1,5},{2,6},{3,7},{4,8},{5,9},{6,10},{7,11},{8,12},{9,13},{1... | collective-permute-start | bytes 786440 | tf_op jit(solution)/shard_map/ppermute | solution.py:15
  83.5 24.7 %collective-permute-start.3 = (bf16[128,1024]{1,0:T(8,128)(2,1)S(1)}, bf16[128,1024]{1,0:T(8,128)(2,1)}, u32[]{:S(2)}, u32[]{:S(2)}) collective-permute-start(bf16[128,1024]{1,0:T(8,128)(2,1)S(1)} %copy-done.9), channel_id=1, source_target_pairs={{0,1},{1,2},{2,3},{3,4},{4,5},{5,6},{6,7},{7,8},{8,9},{9,10},{10,1... | collective-permute-start | bytes 786440 | tf_op jit(solution)/shard_map/ppermute | solution.py:15
  102.3 11.0 %copy-start.3 = (bf16[640,8,128]{0,2,1:T(8,128)(2,1)S(1)}, bf16[640,8,128]{0,2,1:T(8,128)(2,1)}, u32[]{:S(2)}) copy-start(bf16[640,8,128]{0,2,1:T(8,128)(2,1)} %copy.67) | copy-start | bytes 3932164
  125.8 5.4 %copy-start.4 = (bf16[640,8,128]{2,0,1:T(8,128)(2,1)S(1)}, bf16[640,8,128]{2,0,1:T(8,128)(2,1)}, u32[]{:S(2)}) copy-start(bf16[640,8,128]{2,0,1:T(8,128)(2,1)} %copy_bitcast_fusion) | copy-start | bytes 3932164
  131.2 1.2 copy-start.5
  135.5 10.2 %slice-start = ((s8[5242880]{0:T(1024)(128)(4,1)}), s8[1048576]{0:T(1024)(128)(4,1)S(1)}, s32[]{:S(2)}) async-start(s8[5242880]{0:T(1024)(128)(4,1)} %bitcast.118), calls=%async_computation | async-start | bytes 2097152
  138.9 6.8 %slice-start.1 = ((s8[5242880]{0:T(1024)(128)(4,1)}), s8[4194304]{0:T(1024)(128)(4,1)S(1)}, s32[]{:S(2)}) async-start(s8[5242880]{0:T(1024)(128)(4,1)} %bitcast.118), calls=%async_computation.1 | async-start | bytes 8388608
  145.7 4.1 copy-start.2
  156.2 4.7 %copy-start = (f32[640,8,128]{0,2,1:T(8,128)S(1)}, f32[640,8,128]{0,2,1:T(8,128)}, u32[]{:S(2)}) copy-start(f32[640,8,128]{0,2,1:T(8,128)} %bitcast_reduce_fusion.1) | copy-start | bytes 7864324
  160.9 23.3 %copy-start.6 = (f32[640,8,128]{2,0,1:T(8,128)S(1)}, f32[640,8,128]{2,0,1:T(8,128)}, u32[]{:S(2)}) copy-start(f32[640,8,128]{2,0,1:T(8,128)} %bitcast_reduce_fusion) | copy-start | bytes 7864324
  161.4 29.5 %collective-permute-start.8 = (bf16[128,8,128]{0,2,1:T(8,128)(2,1)S(1)}, bf16[128,8,128]{0,2,1:T(8,128)(2,1)S(1)}, u32[]{:S(2)}, u32[]{:S(2)}) collective-permute-start(bf16[128,8,128]{0,2,1:T(8,128)(2,1)S(1)} %get-tuple-element.81), channel_id=1, source_target_pairs={{4,0},{5,1},{6,2},{7,3},{8,4},{9,5},{10,6},{11,7},{12,8},{13,9},{1... | collective-permute-start | bytes 786440 | tf_op jit(solution)/shard_map/ppermute | solution.py:15
  165.7 27.1 %collective-permute-start.11 = (bf16[128,8,128]{0,2,1:T(8,128)(2,1)S(1)}, bf16[128,8,128]{0,2,1:T(8,128)(2,1)S(1)}, u32[]{:S(2)}, u32[]{:S(2)}) collective-permute-start(bf16[128,8,128]{0,2,1:T(8,128)(2,1)S(1)} %get-tuple-element.82), channel_id=1, source_target_pairs={{1,0},{2,1},{3,2},{4,3},{5,4},{6,5},{7,6},{8,7},{9,8},{10,9},{11,1... | collective-permute-start | bytes 786440 | tf_op jit(solution)/shard_map/ppermute | solution.py:15
  169.4 29.5 %collective-permute-start.10 = (bf16[128,8,128]{0,2,1:T(8,128)(2,1)S(1)}, bf16[128,8,128]{0,2,1:T(8,128)(2,1)S(1)}, u32[]{:S(2)}, u32[]{:S(2)}) collective-permute-start(bf16[128,8,128]{0,2,1:T(8,128)(2,1)S(1)} %get-tuple-element.83), channel_id=1, source_target_pairs={{2,0},{3,1},{4,2},{5,3},{6,4},{7,5},{8,6},{9,7},{10,8},{11,9},{12,... | collective-permute-start | bytes 786440 | tf_op jit(solution)/shard_map/ppermute | solution.py:15
  178.2 11.6 %copy-start.1 = (f32[128,32,128]{0,2,1:T(8,128)S(1)}, f32[128,32,128]{0,2,1:T(8,128)}, u32[]{:S(2)}) copy-start(f32[128,32,128]{0,2,1:T(8,128)} %get-tuple-element.75) | copy-start | bytes 6291460
  178.2 11.6 %copy-start.11 = (s32[128]{0:T(128)S(1)}, s32[128]{0:T(128)}, u32[]{:S(2)}) copy-start(s32[128]{0:T(128)} %param.11) | copy-start | bytes 1540
  178.2 38.9 %collective-permute-start.9 = (bf16[128,8,128]{0,2,1:T(8,128)(2,1)S(1)}, bf16[128,8,128]{0,2,1:T(8,128)(2,1)S(1)}, u32[]{:S(2)}, u32[]{:S(2)}) collective-permute-start(bf16[128,8,128]{0,2,1:T(8,128)(2,1)S(1)} %get-tuple-element.84), channel_id=1, source_target_pairs={{3,0},{4,1},{5,2},{6,3},{7,4},{8,5},{9,6},{10,7},{11,8},{12,9},{13... | collective-permute-start | bytes 786440 | tf_op jit(solution)/shard_map/ppermute | solution.py:15
  185.4 34.7 %collective-permute-start.12 = (bf16[128,8,128]{2,0,1:T(8,128)(2,1)}, bf16[128,8,128]{2,0,1:T(8,128)(2,1)S(1)}, u32[]{:S(2)}, u32[]{:S(2)}) collective-permute-start(bf16[128,8,128]{2,0,1:T(8,128)(2,1)} %get-tuple-element.77), channel_id=1, source_target_pairs={{4,0},{5,1},{6,2},{7,3},{8,4},{9,5},{10,6},{11,7},{12,8},{13,9},{1... | collective-permute-start | bytes 786440 | tf_op jit(solution)/shard_map/ppermute | solution.py:15
  190.9 29.2 %collective-permute-start.15 = (bf16[128,8,128]{2,0,1:T(8,128)(2,1)}, bf16[128,8,128]{2,0,1:T(8,128)(2,1)}, u32[]{:S(2)}, u32[]{:S(2)}) collective-permute-start(bf16[128,8,128]{2,0,1:T(8,128)(2,1)} %get-tuple-element.78), channel_id=1, source_target_pairs={{1,0},{2,1},{3,2},{4,3},{5,4},{6,5},{7,6},{8,7},{9,8},{10,9},{11,1... | collective-permute-start | bytes 786440 | tf_op jit(solution)/shard_map/ppermute | solution.py:15
  192.8 39.0 %collective-permute-start.14 = (bf16[128,8,128]{2,0,1:T(8,128)(2,1)}, bf16[128,8,128]{2,0,1:T(8,128)(2,1)}, u32[]{:S(2)}, u32[]{:S(2)}) collective-permute-start(bf16[128,8,128]{2,0,1:T(8,128)(2,1)} %get-tuple-element.79), channel_id=1, source_target_pairs={{2,0},{3,1},{4,2},{5,3},{6,4},{7,5},{8,6},{9,7},{10,8},{11,9},{12,... | collective-permute-start | bytes 786440 | tf_op jit(solution)/shard_map/ppermute | solution.py:15
  198.9 47.2 %collective-permute-start.13 = (bf16[128,8,128]{2,0,1:T(8,128)(2,1)}, bf16[128,8,128]{2,0,1:T(8,128)(2,1)}, u32[]{:S(2)}, u32[]{:S(2)}) collective-permute-start(bf16[128,8,128]{2,0,1:T(8,128)(2,1)} %get-tuple-element.80), channel_id=1, source_target_pairs={{3,0},{4,1},{5,2},{6,3},{7,4},{8,5},{9,6},{10,7},{11,8},{12,9},{13... | collective-permute-start | bytes 786440 | tf_op jit(solution)/shard_map/ppermute | solution.py:15
  218.1 1.6 copy-start.7
